TPU v7x, 512 devices: a whole 4x4x16 slice. The times are simulated.
512 devices in a mesh: group: 8 (over x_hi, y), fsdp: 64 (over x_lo, z, core).
Axes of the slice: x: 4 (x_hi: 2, x_lo: 2; x = x_hi * 2 + x_lo), y: 4, z: 16, core: 2. Of those that a mesh axis runs over, the one named last changes fastest.
Arguments:
- gossip_step: int32 [1], replicated, may hold values from 0 to 199
- context: bfloat16 [8, 24576, 256], P('group', 'fsdp'), may hold values from -6 to 6
- upstream: bfloat16 [8, 24576, 4096], P('group', 'fsdp'), may hold values from -3 to 3
- master: float32 [8, 8192, 128], P('group', 'fsdp'), may hold values from -0.375 to 0.375
- moment_one: float32 [8, 8192, 128], P('group', 'fsdp'), may hold values from -3 to 3
- moment_two: float32 [8, 8192, 128], P('group', 'fsdp'), may hold values from 0.0001 to 0.01
Outputs:
- context_grad: bfloat16 [8, 24576, 256], P('group', 'fsdp')
- master_out: float32 [8, 8192, 128], P('group', 'fsdp')
- moment_one_out: float32 [8, 8192, 128], P('group', 'fsdp')
- moment_two_out: float32 [8, 8192, 128], P('group', 'fsdp')
All inputs are finite; a program needn't handle non-finite values.
Results may differ from a plain program's by a relative error of at most 0.0049.
Values may be sent and summed in bfloat16 or wider, within the bound.
A program may use at most 64 MiB of HBM per device.

v0:
```python
import math

import jax
import jax.numpy as jnp
from jax import lax
from jax.sharding import PartitionSpec as P

D = 4096
ROWS = 256


beta_one = 0.9
beta_two = 0.999
adam_eps = 1e-08
learn_rate = 0.003
decay_rate = 0.1


def partner_2(value, axis, apart):
    mask = 2**apart
    pairs = [(source, source ^ mask) for source in range(lax.axis_size(axis))]
    return lax.ppermute(value, axis, pairs)


def shards(gossip_step, context, upstream, master, moment_one, moment_two):
    ctx_rows = context[0]
    grad_rows = upstream[0]
    shard = master[0]
    gathered = lax.all_gather(shard.astype(jnp.bfloat16), "fsdp", axis=0, tiled=True)
    weight = gathered.reshape(ROWS, D)
    context_grad = lax.dot_general(
        grad_rows, weight, (((1,), (1,)), ((), ())), preferred_element_type=jnp.float32
    ).astype(jnp.bfloat16)
    tokens = grad_rows.shape[0] * lax.axis_size("fsdp")
    scale = 1.0 / math.sqrt(tokens)
    partial_sum = lax.dot_general(
        ctx_rows, grad_rows, (((0,), (0,)), ((), ())), preferred_element_type=jnp.float32
    )
    summed = lax.psum_scatter(partial_sum.reshape(-1, 128), "fsdp", scatter_dimension=0, tiled=True)
    gradient = summed * scale
    step_number = (gossip_step[0] + 1).astype(jnp.float32)
    first_moment = beta_one * moment_one[0] + (1.0 - beta_one) * gradient
    second_moment = beta_two * moment_two[0] + (1.0 - beta_two) * gradient * gradient
    fix_one = 1.0 - jnp.power(jnp.float32(beta_one), step_number)
    fix_two = 1.0 - jnp.power(jnp.float32(beta_two), step_number)
    update = first_moment / fix_one / (jnp.sqrt(second_moment / fix_two) + adam_eps)
    stepped = shard - learn_rate * (update + decay_rate * shard)
    bit_count = lax.axis_size("group").bit_length() - 1
    chosen = gossip_step[0] % bit_count
    partner = stepped
    for level in range(bit_count):
        received = partner_2(stepped.astype(jnp.bfloat16), "group", level).astype(stepped.dtype)
        partner = jnp.where(chosen == level, received, partner)
    averaged = 0.5 * (stepped + partner)
    return (context_grad[None], averaged[None], first_moment[None], second_moment[None])


def solution(mesh):
    in_specs = (
        P(),
        P("group", "fsdp", None),
        P("group", "fsdp", None),
        P("group", "fsdp", None),
        P("group", "fsdp", None),
        P("group", "fsdp", None),
    )
    out_specs = (
        P("group", "fsdp", None),
        P("group", "fsdp", None),
        P("group", "fsdp", None),
        P("group", "fsdp", None),
    )
    return jax.shard_map(shards, mesh=mesh, in_specs=in_specs, out_specs=out_specs, check_vma=False)
```

profile of v0, /device:TPU:1, one launch (start us, length us, event | category | flops | bytes accessed | tf_op | source)
XLA Modules:
  0.0 389.2 jit_solution(5433229598408305406)
XLA Ops:
  7.2 0.0 copy-start
  7.2 0.0 all-gather.2.cloned.1.call-start
  7.2 1.6 bitcast_convert_fusion
  8.8 0.0 all-gather.2.cloned.1.call-update
  8.9 0.0 reduce-scatter.2.cloned.1.call-start
  8.9 0.2 copy-done
  9.1 4.2 %fusion = f32[256,4096]{1,0:T(8,128)} fusion(bf16[1,384,4096]{2,1,0:T(8,128)(2,1)S(1)} %copy-done, bf16[1,384,256]{2,1,0:T(8,128)(2,1)} %param.7), kind=kOutput, calls=%fused_computation | convolution fusion | flops 805306368 | bytes 7536640 | tf_op jit(solution)/shard_map/dot_general | solution.py:36
  13.3 4.9 %reshape.32 = f32[8192,128]{1,0:T(8,128)} reshape(f32[256,4096]{1,0:T(8,128)} %fusion) | data formatting | bytes 8388608 | tf_op jit(solution)/shard_map/reshape | solution.py:39
  18.2 0.0 reduce-scatter.2.cloned.1.call-update
  18.2 0.0 copy-start.1
  18.2 0.0 copy-start.2
  18.2 0.0 copy-start.3
  19.0 119.6 %all-gather.2.cloned.1.call-done = bf16[8192,128]{1,0:T(8,128)(2,1)} async-done(((bf16[128,128]{1,0:T(8,128)(2,1)}), bf16[8192,128]{1,0:T(8,128)(2,1)}) %all-gather.2.cloned.1.call-update) | async-done | bytes 2097168 | tf_op jit(solution)/shard_map/all_gather | solution.py:29
  138.6 4.1 %reshape.31 = bf16[256,4096]{1,0:T(8,128)(2,1)} reshape(bf16[8192,128]{1,0:T(8,128)(2,1)} %all-gather.2.cloned.1.call-done) | data formatting | bytes 4194304 | tf_op jit(solution)/shard_map/reshape | solution.py:30
  142.7 222.1 %reduce-scatter.2.cloned.1.call-done = f32[128,128]{1,0:T(8,128)} async-done(((f32[8192,128]{1,0:T(8,128)}), f32[128,128]{1,0:T(8,128)}) %reduce-scatter.2.cloned.1.call-update) | async-done | bytes 65552 | tf_op jit(solution)/shard_map/reduce_scatter | solution.py:39
  364.8 1.5 fusion.15
  366.4 5.2 %collective-permute-start = (bf16[128,128]{1,0:T(8,128)(2,1)S(1)}, bf16[128,128]{1,0:T(8,128)(2,1)S(1)}, u32[]{:S(2)}, u32[]{:S(2)}) collective-permute-start(bf16[128,128]{1,0:T(8,128)(2,1)S(1)} %get-tuple-element.4), channel_id=1, source_target_pairs={{0,256},{64,320},{128,384},{192,448},{256,0},{320,64},{384,128},{4... | collective-permute-start | bytes 98312 | tf_op jit(solution)/shard_map/ppermute | solution.py:22
  371.5 3.8 collective-permute-start.1
  375.3 3.1 collective-permute-start.2
  378.4 3.3 fusion.7
  381.7 0.0 collective-permute-done
  381.7 0.0 collective-permute-done.1
  381.7 0.0 collective-permute-done.2
  381.7 0.7 multiply_bitcast_fusion
  (3 shorter events, 0.0 us)
Async XLA Ops:
  7.2 1.9 copy-start
  7.2 131.4 %all-gather.2.cloned.1.call-start = ((), (), s32[]{:S(2)}) async-start(), calls=%async_computation.1 | async-start | bytes 2129920 | tf_op jit(solution)/shard_map/all_gather | solution.py:29
  8.9 355.9 %reduce-scatter.2.cloned.1.call-start = ((), (), s32[]{:S(2)}) async-start(), calls=%async_computation.2 | async-start | bytes 4259840 | tf_op jit(solution)/shard_map/reduce_scatter | solution.py:39
  18.2 346.6 %copy-start.1 = (f32[1,128,128]{2,1,0:T(8,128)S(1)}, f32[1,128,128]{2,1,0:T(8,128)}, u32[]{:S(2)}) copy-start(f32[1,128,128]{2,1,0:T(8,128)} %param.9) | copy-start | bytes 196612
  18.2 346.6 %copy-start.2 = (f32[1,128,128]{2,1,0:T(8,128)S(1)}, f32[1,128,128]{2,1,0:T(8,128)}, u32[]{:S(2)}) copy-start(f32[1,128,128]{2,1,0:T(8,128)} %param.11) | copy-start | bytes 196612
  18.2 346.6 %copy-start.3 = (f32[1,128,128]{2,1,0:T(8,128)S(1)}, f32[1,128,128]{2,1,0:T(8,128)}, u32[]{:S(2)}) copy-start(f32[1,128,128]{2,1,0:T(8,128)} %param.10) | copy-start | bytes 196612
  366.4 15.3 %collective-permute-start = (bf16[128,128]{1,0:T(8,128)(2,1)S(1)}, bf16[128,128]{1,0:T(8,128)(2,1)S(1)}, u32[]{:S(2)}, u32[]{:S(2)}) collective-permute-start(bf16[128,128]{1,0:T(8,128)(2,1)S(1)} %get-tuple-element.4), channel_id=1, source_target_pairs={{0,256},{64,320},{128,384},{192,448},{256,0},{320,64},{384,128},{4... | collective-permute-start | bytes 98312 | tf_op jit(solution)/shard_map/ppermute | solution.py:22
  371.5 10.2 %collective-permute-start.1 = (bf16[128,128]{1,0:T(8,128)(2,1)S(1)}, bf16[128,128]{1,0:T(8,128)(2,1)S(1)}, u32[]{:S(2)}, u32[]{:S(2)}) collective-permute-start(bf16[128,128]{1,0:T(8,128)(2,1)S(1)} %get-tuple-element.4), channel_id=1, source_target_pairs={{0,128},{64,192},{128,0},{192,64},{256,384},{320,448},{384,256},{4... | collective-permute-start | bytes 98312 | tf_op jit(solution)/shard_map/ppermute | solution.py:22
  375.3 6.4 %collective-permute-start.2 = (bf16[128,128]{1,0:T(8,128)(2,1)S(1)}, bf16[128,128]{1,0:T(8,128)(2,1)S(1)}, u32[]{:S(2)}, u32[]{:S(2)}) collective-permute-start(bf16[128,128]{1,0:T(8,128)(2,1)S(1)} %get-tuple-element.4), channel_id=1, source_target_pairs={{0,64},{64,0},{128,192},{192,128},{256,320},{320,256},{384,448},{4... | collective-permute-start | bytes 98312 | tf_op jit(solution)/shard_map/ppermute | solution.py:22
Sparse Core Ops, SparseCore 0:
  10.7 127.7 all-gather.1
  141.4 223.3 reduce-scatter.1
where the time goes:
time: 393 us; the launch traced here: 389 us
  waiting for transfers between devices  342 us (87%)
  between operations  14.9 us (4%)
  starting transfers between devices  12.1 us (3%)
  local copies, waits for them, and re-layouts  9.24 us (2%)
  matrix products  7.45 us (2%)
    reduce_scatter x1, waiting for transfers between devices, shards(): lax.psum_scatter(partial_sum.reshape(-1, 128), 'fsdp', scatter_dimension=...  222 us
    all_gather x1, waiting for transfers between devices, shards(): lax.all_gather(shard.astype(jnp.bfloat16), 'fsdp', axis=0, tiled=True)  120 us
    ppermute x3, starting transfers between devices, partner_2(): return lax.ppermute(value, axis, pairs)  12 us
  transfers between devices with their start and end apart: 5, of which 2 were waited for; matrix products, arithmetic and copies ran while one was open for 4% of the time, Pallas kernels for 0%

commit v1 on v0

v1 whole, which is shorter than its diff:
```python
import functools
import math

import jax
import jax.numpy as jnp
from jax import lax
from jax.experimental import pallas as pl
from jax.experimental.pallas import tpu as pltpu
from jax.sharding import PartitionSpec as P

MESH = pl.DeviceIdType.MESH
BF16 = jnp.bfloat16
F32 = jnp.float32

beta_one = 0.9
beta_two = 0.999
adam_eps = 1e-08
learn_rate = 0.003
decay_rate = 0.1

OWN = 4
PARTS = 4
REACH = 2
PIECE = 4


def power_of(base, count):
    total = jnp.full(count.shape, 1.0, F32)
    for bit in range(8):
        factor = jnp.float32(base ** (2**bit))
        total = jnp.where(((count >> bit) & 1) == 1, total * factor, total)
    return total


def kernel(
    NG, Z, tokens_all,
    step_ref, ctx_hbm, up_hbm, master_hbm, one_hbm, two_hbm,
    grad_hbm, master_out_hbm, one_out_hbm, two_out_hbm,
    ctx, up, master, one, two,
    gsum, own, csend, crecv, xsend, xrecv, zsend, zrecv,
    wbuf, wmat, cg, folded, stepped, sent, got,
    grad_out, master_out, one_out, two_out,
    in_sem, out_sem,
    azs, azr, axs, axr, acs, acr,
    rcs, rcr, rxs, rxr, rzs, rzr, gs, gr,
):
    T, D = up.shape
    Q = D // PARTS
    KK = Q // 128
    half = Z // 2
    bits = NG.bit_length() - 1
    group = lax.axis_index("group")
    index = lax.axis_index("fsdp")
    x = index // (2 * Z)
    z = lax.rem(index // 2, Z)
    c = lax.rem(index, 2)

    def at(x_, z_, c_):
        return (group, x_ * (2 * Z) + z_ * 2 + c_)

    def along(k):
        return at(x, lax.rem(z + (k + 2 * Z), Z), c)

    over = at(1 - x, z, c)
    beside = at(x, z, 1 - c)
    partners = [(jnp.bitwise_xor(group, 1 << b), index) for b in range(bits)]

    loads = {}

    def load(name, src, dst, n):
        copy = pltpu.make_async_copy(src, dst, in_sem.at[n])
        copy.start()
        loads[name] = copy

    load("master", master_hbm, master, 0)
    load("ctx", ctx_hbm, ctx, 1)
    for q in range(PARTS):
        load(("up", q), up_hbm.at[:, pl.ds(q * Q, Q)], up.at[:, pl.ds(q * Q, Q)], 2 + q)
    load("one", one_hbm, one, 2 + PARTS)
    load("two", two_hbm, two, 3 + PARTS)

    reach = min(REACH, half)
    hops = sorted({h % Z for h in range(1, reach + 1)} | {-h % Z for h in range(1, reach + 1)})
    peers = [along(h) for h in hops] + [over, beside] + partners
    barrier = pltpu.get_barrier_semaphore()
    for peer in peers:
        pl.semaphore_signal(barrier, inc=1, device_id=peer, device_id_type=MESH)

    started = []

    def send(copy):
        copy.start()
        started.append(copy)

    def remote(src, dst, ss, rs, to):
        return pltpu.make_async_remote_copy(
            src_ref=src, dst_ref=dst, send_sem=ss, recv_sem=rs, device_id=to, device_id_type=MESH
        )

    row8 = lax.broadcasted_iota(jnp.int32, (8, Q), 0)
    low = row8 < OWN

    def turn(value):
        return pltpu.roll(value, 4, 0)

    def z_of(k):
        return lax.rem(z + (2 * Z - k), Z)

    def a_z(k, hop):
        chunk = wbuf.at[x, c, z_of(k - hop)]
        there = k % Z
        return remote(chunk, chunk, azs.at[there], azr.at[there], along(hop))

    def a_x(k):
        chunk = wbuf.at[x, c, z_of(k)]
        return remote(chunk, chunk, axs.at[k % Z], axr.at[k % Z], over)

    def a_c(w, k):
        chunk = wbuf.at[x if w == 0 else 1 - x, c, z_of(k)]
        return remote(chunk, chunk, acs.at[w, k % Z], acr.at[w, k % Z], beside)

    def arrived_z(k):
        chunk = wbuf.at[x, c, z_of(k)]
        remote(chunk, chunk, azs.at[k % Z], azr.at[k % Z], over).wait_recv()

    def arrived_x(k):
        chunk = wbuf.at[1 - x, c, z_of(k)]
        remote(chunk, chunk, axs.at[k % Z], axr.at[k % Z], over).wait_recv()

    def arrived_c(w, k):
        chunk = wbuf.at[x if w == 0 else 1 - x, 1 - c, z_of(k)]
        remote(chunk, chunk, acs.at[w, k % Z], acr.at[w, k % Z], beside).wait_recv()

    plus = list(range(1, half + 1))
    minus = [-k for k in range(1, half)]

    def a_forward(k):
        if k >= 0 and k % reach == 0:
            for hop in range(reach, 0, -1):
                if k + hop <= half:
                    send(a_z(k + hop, hop))
        if k <= 0 and (-k) % reach == 0:
            for hop in range(reach, 0, -1):
                if -k + hop <= half - 1:
                    send(a_z(k - hop, -hop))

    def make_chunk():
        loads["master"].wait()
        for q in range(PARTS):
            for r in range(OWN):
                folded[pl.ds((q * OWN + r) * KK, KK), :] = master[pl.ds((r * PARTS + q) * KK, KK), :]
        for k in range(KK):
            wbuf[x, c, z, :, pl.ds(k * 128, 128)] = folded[pl.ds(k, 16, stride=KK), :].astype(BF16)

    def a_start():
        a_forward(0)
        send(a_x(0))
        send(a_c(0, 0))

    def a_got_z(k):
        arrived_z(k)
        a_forward(k)
        send(a_x(k))
        send(a_c(0, k))

    def a_got_x(k):
        arrived_x(k)
        send(a_c(1, k))

    def a_got_c(k):
        arrived_c(0, k)
        arrived_c(1, k)

    def unfold(j):
        pair = lax.rem(z // 2 + (j + Z), half)

        for x_ in range(2):
            outs = [[] for _ in range(PARTS)]
            for side in range(2):
                first = wbuf[x_, 0, 2 * pair + side].astype(F32)
                second = wbuf[x_, 1, 2 * pair + side].astype(F32)
                for h in range(2):
                    a = first[8 * h : 8 * h + 8]
                    b = second[8 * h : 8 * h + 8]
                    outs[2 * h].append(jnp.where(low, a, turn(b)))
                    outs[2 * h + 1].append(jnp.where(low, turn(a), b))
            start = pl.multiple_of(x_ * (8 * Z) + pair * 16, 16)
            for q in range(PARTS):
                wmat[pl.ds(start, 16), pl.ds(q * Q, Q)] = jnp.concatenate(outs[q], 0).astype(BF16)

    def multiply():
        for q in range(PARTS):
            part = lax.dot_general(
                up[:, pl.ds(q * Q, Q)], wmat[:, pl.ds(q * Q, Q)],
                (((1,), (1,)), ((), ())), preferred_element_type=F32,
            )
            if q == 0:
                cg[...] = part
            elif q < PARTS - 1:
                cg[...] += part
            else:
                grad_out[...] = (cg[...] + part).astype(BF16)
        copy = pltpu.make_async_copy(grad_out, grad_hbm, out_sem.at[0])
        copy.start()
        started_out.append(copy)

    started_out = []

    def offset(j):
        return jnp.where(lax.rem(j, 2) == 1, half - (j + 1) // 2, (j // 2) - half)

    order = [half]
    for k in range(half - 1, 0, -1):
        order += [k, -k]
    order.append(0)
    place = {k: j for j, k in enumerate(order)}

    def product():
        loads["ctx"].wait()
        turned = ctx[...].T
        for q in range(PARTS):
            loads[("up", q)].wait()
            gsum[q] = jnp.dot(turned, up[:, pl.ds(q * Q, Q)], preferred_element_type=F32)

    first_core = c == 0

    def fold(w, j):
        z_ = lax.rem(z + (offset(j) + Z), Z)
        x_ = 1 - x if w == 0 else x
        start = pl.multiple_of(x_ * (8 * Z) + z_ * 8, 8)
        s = [gsum[q, pl.ds(start, 8), :] for q in range(PARTS)]
        t = [turn(v) for v in s]
        for h in range(2):
            zero = jnp.where(low, s[2 * h], t[2 * h + 1])
            next_ = jnp.where(low, t[2 * h], s[2 * h + 1])
            own[w, j, pl.ds(8 * h, 8), :] = jnp.where(first_core, zero, next_)
            folded2[h] = jnp.where(first_core, next_, zero)
        csend[w, j] = jnp.concatenate([folded2[0], folded2[1]], 0).astype(BF16)

    folded2 = [None, None]
    pieces = Z // PIECE

    def r_c(w, p):
        part = pl.ds(p * PIECE, PIECE)
        return remote(csend.at[w, part], crecv.at[w, part], rcs.at[w, p], rcr.at[w, p], beside)

    def r_fold(w, p):
        def body(j, carry):
            fold(w, j)
            return carry

        lax.fori_loop(p * PIECE, (p + 1) * PIECE, body, 0)
        send(r_c(w, p))

    def r_x(j):
        return remote(xsend.at[j], xrecv.at[j], rxs.at[j], rxr.at[j], over)

    def r_over(p):
        r_c(0, p).wait_recv()
        for j in range(p * PIECE, (p + 1) * PIECE):
            xsend[j] = (own[0, j] + crecv[0, j].astype(F32)).astype(BF16)
            send(r_x(j))

    def hop_of(k):
        size = abs(k)
        step = (size - 1) % reach + 1
        return step if k > 0 else -step

    def r_z(k):
        return remote(zsend.at[k % Z], zrecv.at[k % Z], rzs.at[k % Z], rzr.at[k % Z], along(hop_of(k)))

    waited = set()

    def feeds(k):
        out = []
        for k_ in plus + minus:
            if k_ - hop_of(k_) == k:
                out.append(k_)
        return out

    def r_sum(k):
        j = place[k]
        p = j // PIECE
        if ("c", p) not in waited:
            waited.add(("c", p))
            r_c(1, p).wait_recv()
        r_x(j).wait_recv()
        total = own[1, j] + crecv[1, j].astype(F32) + xrecv[j].astype(F32)
        for k_ in feeds(k):
            r_z(k_).wait_recv()
            total += zrecv[k_ % Z].astype(F32)
        return total

    def r_send(k):
        zsend[k % Z] = r_sum(k).astype(BF16)
        send(r_z(k))

    def finish():
        total = r_sum(0)
        loads["one"].wait()
        loads["two"].wait()
        scale = 1.0 / math.sqrt(tokens_all)
        for k in range(KK):
            folded[pl.ds(k, 16, stride=KK), :] = total[:, k * 128 : (k + 1) * 128]
        count = jnp.full((KK, 128), step_ref[0] + 1, jnp.int32)
        fix_one = 1.0 - power_of(beta_one, count)
        fix_two = 1.0 - power_of(beta_two, count)
        pair = []
        for b in range(16):
            q, r = b // OWN, b % OWN
            here = pl.ds((r * PARTS + q) * KK, KK)
            gradient = folded[pl.ds(b * KK, KK), :] * scale
            shard = master[here, :]
            first = beta_one * one[here, :] + (1.0 - beta_one) * gradient
            second = beta_two * two[here, :] + (1.0 - beta_two) * gradient * gradient
            update = first / fix_one / (jnp.sqrt(second / fix_two) + adam_eps)
            new = shard - learn_rate * (update + decay_rate * shard)
            one_out[here, :] = first
            two_out[here, :] = second
            stepped[pl.ds(b * KK, KK), :] = new
            pair.append(new)
            if b % 2 == 1:
                sent[pl.ds((b - 1) * KK, 2 * KK), :] = jnp.concatenate(pair, 0).astype(BF16)
                pair = []
        for b in range(bits):
            send(gossip(b))
        for n, (src, dst) in enumerate(((one_out, one_out_hbm), (two_out, two_out_hbm))):
            copy = pltpu.make_async_copy(src, dst, out_sem.at[1 + n])
            copy.start()
            started_out.append(copy)

    def gossip(b):
        return remote(sent, got.at[b], gs.at[b], gr.at[b], partners[b])

    def average():
        for b in range(bits):
            gossip(b).wait_recv()
        chosen = jnp.full((2 * KK, 128), lax.rem(step_ref[0], bits), jnp.int32)
        for n in range(8):
            here = pl.ds(n * 2 * KK, 2 * KK)
            other = got[0, here, :].astype(F32)
            for b in range(1, bits):
                other = jnp.where(chosen == b, got[b, here, :].astype(F32), other)
            mean = 0.5 * (stepped[here, :] + other)
            for s in range(2):
                b = 2 * n + s
                q, r = b // OWN, b % OWN
                master_out[pl.ds((r * PARTS + q) * KK, KK), :] = mean[s * KK : (s + 1) * KK]
        copy = pltpu.make_async_copy(master_out, master_out_hbm, out_sem.at[3])
        copy.start()
        started_out.append(copy)

    make_chunk()
    pl.semaphore_wait(barrier, len(peers))
    a_start()
    product()
    for w in range(2):
        for p in range(pieces):
            r_fold(w, p)

    events = []

    def add(time, what, *args):
        events.append((time, len(events), what, args))

    step_time = 3.6 if reach <= 2 else 5.0
    x_time = 1.0
    z_ready = {0: 2.0}
    for k in plus + minus:
        ready = 2.0 + step_time * (-(-abs(k) // reach)) + 0.1 * abs(k)
        z_ready[k] = ready
        add(ready, a_got_z, k)
    c_ready = {}
    for k in [0] + plus + minus:
        ready = z_ready[k] + 4.5
        add(ready, a_got_x, k)
        c_ready[k] = ready + 2.0
        add(c_ready[k], a_got_c, k) if k else add(c_ready[k], arrived_c, 1, 0)
    add(c_ready[0] - 0.5, arrived_c, 0, 0)
    last = 0.0
    for j in range(half):
        rel = j if j <= half // 2 else j - half
        ks = {(-(2 * rel + d)) % Z for d in (-1, 0, 1)}
        ready = max(c_ready[k] for k in c_ready if k % Z in ks) + 0.2
        last = max(last, ready)
        add(ready, unfold, rel)
    r_ready = {}
    for p in range(pieces):
        add(5.0 + 0.3 * p, r_over, p)
    for k in order:
        ready = 8.0 + x_time * place[k]
        for k_ in feeds(k):
            ready = max(ready, r_ready[k_] + step_time)
        r_ready[k] = ready
        if k:
            add(ready, r_send, k)
    add(r_ready[0], finish)
    add(last + 0.1, multiply)
    add(max(r_ready[0] + 4.0, last + 1.0), average)
    for _, _, what, args in sorted(events, key=lambda e: e[:2]):
        what(*args)
    for copy in started_out:
        copy.wait()
    for copy in started:
        copy.wait_send()


def shards(NG, NF, tokens_all, gossip_step, context, upstream, master, moment_one, moment_two):
    Z = NF // 4
    T, rows = context.shape[1:]
    D = upstream.shape[2]
    flat = master.shape[1]
    Q = D // PARTS
    bits = NG.bit_length() - 1
    DMA = pltpu.SemaphoreType.DMA
    V = pltpu.VMEM
    chunk = (16, Q)
    any_ = pl.BlockSpec(memory_space=pl.ANY)
    shard = jax.ShapeDtypeStruct((flat, 128), F32)
    outs = pl.pallas_call(
        functools.partial(kernel, NG, Z, tokens_all),
        out_shape=(jax.ShapeDtypeStruct((T, rows), BF16), shard, shard, shard),
        in_specs=[pl.BlockSpec(memory_space=pltpu.SMEM)] + [any_] * 5,
        out_specs=(any_,) * 4,
        scratch_shapes=[
            V((T, rows), BF16), V((T, D), BF16), V((flat, 128), F32), V((flat, 128), F32), V((flat, 128), F32),
            V((PARTS, rows, Q), F32), V((2, Z) + chunk, F32), V((2, Z) + chunk, BF16), V((2, Z) + chunk, BF16),
            V((Z,) + chunk, BF16), V((Z,) + chunk, BF16), V((Z,) + chunk, BF16), V((Z,) + chunk, BF16),
            V((2, 2, Z) + chunk, BF16), V((rows, D), BF16), V((T, rows), F32),
            V((flat, 128), F32), V((flat, 128), F32), V((flat, 128), BF16), V((bits, flat, 128), BF16),
            V((T, rows), BF16), V((flat, 128), F32), V((flat, 128), F32), V((flat, 128), F32),
            DMA((4 + PARTS,)), DMA((4,)),
            DMA((Z,)), DMA((Z,)), DMA((Z,)), DMA((Z,)), DMA((2, Z)), DMA((2, Z)),
            DMA((2, Z // PIECE)), DMA((2, Z // PIECE)), DMA((Z,)), DMA((Z,)), DMA((Z,)), DMA((Z,)),
            DMA((bits,)), DMA((bits,)),
        ],
        compiler_params=pltpu.CompilerParams(
            collective_id=0, has_side_effects=True, vmem_limit_bytes=40 * 1024 * 1024
        ),
        name="step",
    )(gossip_step, context[0], upstream[0], master[0], moment_one[0], moment_two[0])
    return tuple(out[None] for out in outs)


def solution(mesh):
    whole = P("group", "fsdp", None)

    def run(gossip_step, context, upstream, master, moment_one, moment_two):
        body = functools.partial(shards, mesh.shape["group"], mesh.shape["fsdp"], context.shape[1])
        return jax.shard_map(
            body, mesh=mesh, in_specs=(P(),) + (whole,) * 5, out_specs=(whole,) * 4, check_vma=False
        )(gossip_step, context, upstream, master, moment_one, moment_two)

    return run
```

time: 393 us -> 62.1 us (0.16)
  waiting for transfers between devices: 342 us -> 0 us
  Pallas kernels: 0 us -> 52.6 us
  between operations: 14.9 us -> 1.3 us
  starting transfers between devices: 12.1 us -> 0 us
  matrix products: 7.45 us -> 0 us
    reduce_scatter x1 -> x0, waiting for transfers between devices: 222 us -> none  [shards(): lax.psum_scatter(partial_sum.reshape(-1, 128), 'fsdp', scatter_dimension=...]
    all_gather x1 -> x0, waiting for transfers between devices: 120 us -> none  [shards(): lax.all_gather(shard.astype(jnp.bfloat16), 'fsdp', axis=0, tiled=True)]
    pallas_call x0 -> x1, Pallas kernels: none -> 52.6 us  [shards(): pl.pallas_call(functools.partial(kernel, NG, Z, tokens_all), out_shape=(j...]
    ppermute x3 -> x0, starting transfers between devices: 12 us -> none  [partner_2(): return lax.ppermute(value, axis, pairs)]
    reshape x2 -> x0, local copies, waits for them, and re-layouts: 9.04 us -> none  [the longest x1 4.89 us: shards(): partial_sum.reshape(-1, 128)]
    unnamed x8 -> x14, local copies, waits for them, and re-layouts: 0.21 us -> 7.89 us
    dot_general x2 -> x0, matrix products: 7.45 us -> none  [the longest x1 4.17 us: shards(): lax.dot_general(ctx_rows, grad_rows, (((0,), (0,)), ((), ())), preferred_...]
  transfers between devices with their start and end apart: 5 -> 0, of which waited for: 2 -> 0; matrix products, arithmetic and copies ran while one was open for 4% -> 0% of each run, Pallas kernels for 0% -> 0%
where the time goes in v1:
time: 62.1 us; the launch traced here: 61.8 us
  Pallas kernels  52.6 us (85%)
  local copies, waits for them, and re-layouts  7.89 us (13%)
  between operations  1.3 us (2%)
    pallas_call x1, Pallas kernels, shards(): pl.pallas_call(functools.partial(kernel, NG, Z, tokens_all), out_shape=(j...  52.6 us
    unnamed x14, local copies, waits for them, and re-layouts  7.89 us

profile of v1, /device:TPU:1, one launch (start us, length us, event | category | flops | bytes accessed | tf_op | source)
XLA Modules:
  0.0 61.8 jit_solution(11769825612810528429)
XLA Ops:
  1.3 0.0 copy-start
  1.3 1.9 %copy-done = bf16[1,384,4096]{2,1,0:T(8,128)(2,1)S(1)} copy-done((bf16[1,384,4096]{2,1,0:T(8,128)(2,1)S(1)}, bf16[1,384,4096]{2,1,0:T(8,128)(2,1)}, u32[]{:S(2)}) %copy-start) | copy-done | bytes 3145752
  3.2 0.0 copy-start.1
  3.2 0.9 %copy-done.1 = bf16[1,384,256]{2,1,0:T(8,128)(2,1)S(1)} copy-done((bf16[1,384,256]{2,1,0:T(8,128)(2,1)S(1)}, bf16[1,384,256]{2,1,0:T(8,128)(2,1)}, u32[]{:S(2)}) %copy-start.1) | copy-done | bytes 196632
  4.1 0.0 copy-start.2
  4.1 0.8 %copy-done.2 = f32[1,128,128]{2,1,0:T(8,128)S(1)} copy-done((f32[1,128,128]{2,1,0:T(8,128)S(1)}, f32[1,128,128]{2,1,0:T(8,128)}, u32[]{:S(2)}) %copy-start.2) | copy-done | bytes 65560
  4.9 0.0 copy-start.3
  4.9 0.8 %copy-done.3 = f32[1,128,128]{2,1,0:T(8,128)S(1)} copy-done((f32[1,128,128]{2,1,0:T(8,128)S(1)}, f32[1,128,128]{2,1,0:T(8,128)}, u32[]{:S(2)}) %copy-start.3) | copy-done | bytes 65560
  5.8 0.0 copy-start.4
  5.8 0.8 %copy-done.4 = f32[1,128,128]{2,1,0:T(8,128)S(1)} copy-done((f32[1,128,128]{2,1,0:T(8,128)S(1)}, f32[1,128,128]{2,1,0:T(8,128)}, u32[]{:S(2)}) %copy-start.4) | copy-done | bytes 65560
  6.6 52.6 %step.1 = (bf16[384,256]{1,0:T(8,128)(2,1)S(1)}, f32[128,128]{1,0:T(8,128)S(1)}, f32[128,128]{1,0:T(8,128)S(1)}, f32[128,128]{1,0:T(8,128)S(1)}) custom-call(s32[1]{0:T(128)S(6)} %copy.14.step_ref, bf16[384,256]{1,0:T(8,128)(2,1)S(1)} %bitcast.11, bf16[384,4096]{1,0:T(8,128)(2,1)S(1)} %bitcast.9, f32[128,128]{1,0:T(8,128)S(1)} %bitcast.15, ...), custom_call_target="tpu_custom_call" | custom-call | tf_op jit(solution)/shard_map/step/pallas_call | solution.py:420
  59.2 0.7 %copy.15 = bf16[1,384,256]{2,1,0:T(8,128)(2,1)} copy(bf16[1,384,256]{2,1,0:T(8,128)(2,1)S(1)} %bitcast.10) | data formatting | bytes 393216
  59.9 0.6 %copy.16 = f32[1,128,128]{2,1,0:T(8,128)} copy(f32[1,128,128]{2,1,0:T(8,128)S(1)} %bitcast.14) | data formatting | bytes 131072
  60.5 0.6 %copy.17 = f32[1,128,128]{2,1,0:T(8,128)} copy(f32[1,128,128]{2,1,0:T(8,128)S(1)} %bitcast.13) | data formatting | bytes 131072
  61.1 0.6 %copy.18 = f32[1,128,128]{2,1,0:T(8,128)} copy(f32[1,128,128]{2,1,0:T(8,128)S(1)} %bitcast.12) | data formatting | bytes 131072
Async XLA Ops:
  1.3 1.9 %copy-start = (bf16[1,384,4096]{2,1,0:T(8,128)(2,1)S(1)}, bf16[1,384,4096]{2,1,0:T(8,128)(2,1)}, u32[]{:S(2)}) copy-start(bf16[1,384,4096]{2,1,0:T(8,128)(2,1)} %param.8) | copy-start | bytes 9437188
  3.2 0.9 %copy-start.1 = (bf16[1,384,256]{2,1,0:T(8,128)(2,1)S(1)}, bf16[1,384,256]{2,1,0:T(8,128)(2,1)}, u32[]{:S(2)}) copy-start(bf16[1,384,256]{2,1,0:T(8,128)(2,1)} %param.7) | copy-start | bytes 589828
  4.1 0.8 %copy-start.2 = (f32[1,128,128]{2,1,0:T(8,128)S(1)}, f32[1,128,128]{2,1,0:T(8,128)}, u32[]{:S(2)}) copy-start(f32[1,128,128]{2,1,0:T(8,128)} %param.9) | copy-start | bytes 196612
  4.9 0.8 %copy-start.3 = (f32[1,128,128]{2,1,0:T(8,128)S(1)}, f32[1,128,128]{2,1,0:T(8,128)}, u32[]{:S(2)}) copy-start(f32[1,128,128]{2,1,0:T(8,128)} %param.10) | copy-start | bytes 196612
  5.8 0.8 %copy-start.4 = (f32[1,128,128]{2,1,0:T(8,128)S(1)}, f32[1,128,128]{2,1,0:T(8,128)}, u32[]{:S(2)}) copy-start(f32[1,128,128]{2,1,0:T(8,128)} %param.11) | copy-start | bytes 196612

commit v2 on v1

--- a/solution.py
+++ b/solution.py
@@ -35,12 +35,11 @@
 def kernel(
     NG, Z, tokens_all,
     step_ref, ctx_hbm, up_hbm, master_hbm, one_hbm, two_hbm,
-    grad_hbm, master_out_hbm, one_out_hbm, two_out_hbm,
+    grad_out, master_out, one_out, two_out,
     ctx, up, master, one, two,
     gsum, own, csend, crecv, xsend, xrecv, zsend, zrecv,
     wbuf, wmat, cg, folded, stepped, sent, got,
-    grad_out, master_out, one_out, two_out,
-    in_sem, out_sem,
+    in_sem,
     azs, azr, axs, axr, acs, acr,
     rcs, rcr, rxs, rxr, rzs, rzr, gs, gr,
 ):
@@ -200,11 +199,6 @@
                 cg[...] += part
             else:
                 grad_out[...] = (cg[...] + part).astype(BF16)
-        copy = pltpu.make_async_copy(grad_out, grad_hbm, out_sem.at[0])
-        copy.start()
-        started_out.append(copy)
-
-    started_out = []
 
     def offset(j):
         return jnp.where(lax.rem(j, 2) == 1, half - (j + 1) // 2, (j // 2) - half)
@@ -250,7 +244,6 @@
             return carry
 
         lax.fori_loop(p * PIECE, (p + 1) * PIECE, body, 0)
-        send(r_c(w, p))
 
     def r_x(j):
         return remote(xsend.at[j], xrecv.at[j], rxs.at[j], rxr.at[j], over)
@@ -324,10 +317,6 @@
                 pair = []
         for b in range(bits):
             send(gossip(b))
-        for n, (src, dst) in enumerate(((one_out, one_out_hbm), (two_out, two_out_hbm))):
-            copy = pltpu.make_async_copy(src, dst, out_sem.at[1 + n])
-            copy.start()
-            started_out.append(copy)
 
     def gossip(b):
         return remote(sent, got.at[b], gs.at[b], gr.at[b], partners[b])
@@ -346,17 +335,17 @@
                 b = 2 * n + s
                 q, r = b // OWN, b % OWN
                 master_out[pl.ds((r * PARTS + q) * KK, KK), :] = mean[s * KK : (s + 1) * KK]
-        copy = pltpu.make_async_copy(master_out, master_out_hbm, out_sem.at[3])
-        copy.start()
-        started_out.append(copy)
 
     make_chunk()
-    pl.semaphore_wait(barrier, len(peers))
-    a_start()
     product()
     for w in range(2):
         for p in range(pieces):
             r_fold(w, p)
+    pl.semaphore_wait(barrier, len(peers))
+    for w in range(2):
+        for p in range(pieces):
+            send(r_c(w, p))
+    a_start()
 
     events = []
 
@@ -399,10 +388,17 @@
     add(max(r_ready[0] + 4.0, last + 1.0), average)
     for _, _, what, args in sorted(events, key=lambda e: e[:2]):
         what(*args)
-    for copy in started_out:
-        copy.wait()
     for copy in started:
         copy.wait_send()
+
+
+def store(*refs):
+    sems = refs[8]
+    copies = [pltpu.make_async_copy(refs[n], refs[4 + n], sems.at[n]) for n in range(4)]
+    for copy in copies:
+        copy.start()
+    for copy in copies:
+        copy.wait()
 
 
 def shards(NG, NF, tokens_all, gossip_step, context, upstream, master, moment_one, moment_two):
@@ -415,30 +411,37 @@
     DMA = pltpu.SemaphoreType.DMA
     V = pltpu.VMEM
     chunk = (16, Q)
-    any_ = pl.BlockSpec(memory_space=pl.ANY)
-    shard = jax.ShapeDtypeStruct((flat, 128), F32)
+    hbm = pl.BlockSpec(memory_space=pltpu.HBM)
+    vmem = pl.BlockSpec(memory_space=pltpu.VMEM)
     outs = pl.pallas_call(
         functools.partial(kernel, NG, Z, tokens_all),
-        out_shape=(jax.ShapeDtypeStruct((T, rows), BF16), shard, shard, shard),
-        in_specs=[pl.BlockSpec(memory_space=pltpu.SMEM)] + [any_] * 5,
-        out_specs=(any_,) * 4,
+        out_shape=(V((T, rows), BF16), V((flat, 128), F32), V((flat, 128), F32), V((flat, 128), F32)),
+        in_specs=[pl.BlockSpec(memory_space=pltpu.SMEM)] + [hbm] * 5,
+        out_specs=(vmem,) * 4,
         scratch_shapes=[
             V((T, rows), BF16), V((T, D), BF16), V((flat, 128), F32), V((flat, 128), F32), V((flat, 128), F32),
             V((PARTS, rows, Q), F32), V((2, Z) + chunk, F32), V((2, Z) + chunk, BF16), V((2, Z) + chunk, BF16),
             V((Z,) + chunk, BF16), V((Z,) + chunk, BF16), V((Z,) + chunk, BF16), V((Z,) + chunk, BF16),
             V((2, 2, Z) + chunk, BF16), V((rows, D), BF16), V((T, rows), F32),
             V((flat, 128), F32), V((flat, 128), F32), V((flat, 128), BF16), V((bits, flat, 128), BF16),
-            V((T, rows), BF16), V((flat, 128), F32), V((flat, 128), F32), V((flat, 128), F32),
-            DMA((4 + PARTS,)), DMA((4,)),
+            DMA((4 + PARTS,)),
             DMA((Z,)), DMA((Z,)), DMA((Z,)), DMA((Z,)), DMA((2, Z)), DMA((2, Z)),
             DMA((2, Z // PIECE)), DMA((2, Z // PIECE)), DMA((Z,)), DMA((Z,)), DMA((Z,)), DMA((Z,)),
             DMA((bits,)), DMA((bits,)),
         ],
         compiler_params=pltpu.CompilerParams(
-            collective_id=0, has_side_effects=True, vmem_limit_bytes=40 * 1024 * 1024
+            collective_id=0, has_side_effects=True, vmem_limit_bytes=60 * 1024 * 1024
         ),
         name="step",
     )(gossip_step, context[0], upstream[0], master[0], moment_one[0], moment_two[0])
+    outs = pl.pallas_call(
+        store,
+        out_shape=tuple(jax.ShapeDtypeStruct(out.shape, out.dtype) for out in outs),
+        in_specs=[vmem] * 4,
+        out_specs=(hbm,) * 4,
+        scratch_shapes=[DMA((4,))],
+        name="store",
+    )(*(pltpu.with_memory_space_constraint(out, pltpu.VMEM) for out in outs))
     return tuple(out[None] for out in outs)
 
 

time: 62.1 us -> 52.5 us (0.85)
  local copies, waits for them, and re-layouts: 7.89 us -> 0 us
  Pallas kernels: 52.6 us -> 50.3 us
    unnamed x14 -> x0, local copies, waits for them, and re-layouts: 7.89 us -> none
    pallas_call x1 -> x2, Pallas kernels: 52.6 us -> 50.3 us  [the longest x1 49.6 us: shards(): pl.pallas_call(functools.partial(kernel, NG, Z, tokens_all), out_shape=(V...]
where the time goes in v2:
time: 52.5 us; the launch traced here: 51.6 us
  Pallas kernels  50.3 us (96%)
  between operations  1.29 us (2%)
    pallas_call x1, Pallas kernels, shards(): pl.pallas_call(functools.partial(kernel, NG, Z, tokens_all), out_shape=(V...  49.6 us

profile of v2, /device:TPU:1, one launch (start us, length us, event | category | flops | bytes accessed | tf_op | source)
XLA Modules:
  0.0 51.6 jit_solution(9462849137481088726)
XLA Ops:
  1.3 49.6 %step.1 = (bf16[384,256]{1,0:T(8,128)(2,1)S(1)}, f32[128,128]{1,0:T(8,128)S(1)}, f32[128,128]{1,0:T(8,128)S(1)}, f32[128,128]{1,0:T(8,128)S(1)}) custom-call(s32[1]{0:T(128)S(6)} %copy.10.step_ref, bf16[384,256]{1,0:T(8,128)(2,1)} %bitcast.10, bf16[384,4096]{1,0:T(8,128)(2,1)} %bitcast.9, f32[128,128]{1,0:T(8,128)} %bitcast.11, f32[128,128]{1,0:T(8,128)} %bitcast.12, ...), custom_call_target="tpu_custom_call" | custom-call | tf_op jit(solution)/shard_map/step/pallas_call | solution.py:416
  50.8 0.8 %store.1 = (bf16[384,256]{1,0:T(8,128)(2,1)}, f32[128,128]{1,0:T(8,128)}, f32[128,128]{1,0:T(8,128)}, f32[128,128]{1,0:T(8,128)}) custom-call(bf16[384,256]{1,0:T(8,128)(2,1)S(1)} %get-tuple-element.12.refs_0_, f32[128,128]{1,0:T(8,128)S(1)} %get-tuple-element.13.refs_1_, f32[128,128]{1,0:T(8,128)S(1)} %get-tuple-element.14.refs_2_, ...), custom_call_target="tpu_custom_call" | custom-call | tf_op jit(solution)/shard_map/store/pallas_call | solution.py:437

commit v3 on v2

--- a/solution.py
+++ b/solution.py
@@ -20,7 +20,23 @@
 
 OWN = 4
 PARTS = 4
-REACH = 2
+WAY_A = {1: 0, 2: 0, 3: 2, 4: 2, 5: 4, 6: 4, 7: 6, 8: 6}
+WAY_R = {1: 0, 2: 0, 3: 0, 4: 3, 5: 3, 6: 3, 7: 6, 8: 6}
+A_STEP = 2.4
+A_HOP = 0.7
+A_OVER = 3.5
+A_BESIDE = 2.0
+A_FIRST = 2.0
+A_CROSS = 0.0
+A_EACH = 0.0
+A_LATE = 18.0
+A_LATER = 0.4
+R_STEP = 2.4
+R_HOP = 0.7
+R_FIRST = 6.5
+R_CHUNK = 0.6
+R_OVER = 3.3
+R_PIECE = 0.2
 PIECE = 4
 
 
@@ -61,6 +77,7 @@
         return at(x, lax.rem(z + (k + 2 * Z), Z), c)
 
     over = at(1 - x, z, c)
+    askew = at(1 - x, z, 1 - c)
     beside = at(x, z, 1 - c)
     partners = [(jnp.bitwise_xor(group, 1 << b), index) for b in range(bits)]
 
@@ -78,9 +95,17 @@
     load("one", one_hbm, one, 2 + PARTS)
     load("two", two_hbm, two, 3 + PARTS)
 
-    reach = min(REACH, half)
-    hops = sorted({h % Z for h in range(1, reach + 1)} | {-h % Z for h in range(1, reach + 1)})
-    peers = [along(h) for h in hops] + [over, beside] + partners
+    plus = list(range(1, half + 1))
+    minus = [-k for k in range(1, half)]
+
+    def before(way, k):
+        return way[k] if k > 0 else -way[-k]
+
+    def after(way, k):
+        return sorted((n for n in plus + minus if before(way, n) == k), key=lambda n: -abs(n))
+
+    hops = sorted({(k - before(way, k)) % Z for way in (WAY_A, WAY_R) for k in plus + minus})
+    peers = [along(h) for h in hops] + [over, askew, beside] + partners
     barrier = pltpu.get_barrier_semaphore()
     for peer in peers:
         pl.semaphore_signal(barrier, inc=1, device_id=peer, device_id_type=MESH)
@@ -110,12 +135,18 @@
         there = k % Z
         return remote(chunk, chunk, azs.at[there], azr.at[there], along(hop))
 
+    def skew(k):
+        return k % 2 == 1
+
     def a_x(k):
         chunk = wbuf.at[x, c, z_of(k)]
-        return remote(chunk, chunk, axs.at[k % Z], axr.at[k % Z], over)
+        return remote(chunk, chunk, axs.at[k % Z], axr.at[k % Z], askew if skew(k) else over)
+
+    def over_chunk(k):
+        return wbuf.at[1 - x, 1 - c if skew(k) else c, z_of(k)]
 
     def a_c(w, k):
-        chunk = wbuf.at[x if w == 0 else 1 - x, c, z_of(k)]
+        chunk = wbuf.at[x, c, z_of(k)] if w == 0 else over_chunk(k)
         return remote(chunk, chunk, acs.at[w, k % Z], acr.at[w, k % Z], beside)
 
     def arrived_z(k):
@@ -123,25 +154,16 @@
         remote(chunk, chunk, azs.at[k % Z], azr.at[k % Z], over).wait_recv()
 
     def arrived_x(k):
-        chunk = wbuf.at[1 - x, c, z_of(k)]
+        chunk = over_chunk(k)
         remote(chunk, chunk, axs.at[k % Z], axr.at[k % Z], over).wait_recv()
 
     def arrived_c(w, k):
-        chunk = wbuf.at[x if w == 0 else 1 - x, 1 - c, z_of(k)]
+        chunk = wbuf.at[x, 1 - c, z_of(k)] if w == 0 else wbuf.at[1 - x, c if skew(k) else 1 - c, z_of(k)]
         remote(chunk, chunk, acs.at[w, k % Z], acr.at[w, k % Z], beside).wait_recv()
 
-    plus = list(range(1, half + 1))
-    minus = [-k for k in range(1, half)]
-
     def a_forward(k):
-        if k >= 0 and k % reach == 0:
-            for hop in range(reach, 0, -1):
-                if k + hop <= half:
-                    send(a_z(k + hop, hop))
-        if k <= 0 and (-k) % reach == 0:
-            for hop in range(reach, 0, -1):
-                if -k + hop <= half - 1:
-                    send(a_z(k - hop, -hop))
+        for n in after(WAY_A, k):
+            send(a_z(n, n - k))
 
     def make_chunk():
         loads["master"].wait()
@@ -153,14 +175,15 @@
 
     def a_start():
         a_forward(0)
-        send(a_x(0))
         send(a_c(0, 0))
 
     def a_got_z(k):
         arrived_z(k)
         a_forward(k)
+        send(a_c(0, k))
+
+    def a_cross(k):
         send(a_x(k))
-        send(a_c(0, k))
 
     def a_got_x(k):
         arrived_x(k)
@@ -216,9 +239,8 @@
             loads[("up", q)].wait()
             gsum[q] = jnp.dot(turned, up[:, pl.ds(q * Q, Q)], preferred_element_type=F32)
 
-    first_core = c == 0
-
     def fold(w, j):
+        first_core = lax.rem(c + j, 2) == 0 if w == 0 else c == 0
         z_ = lax.rem(z + (offset(j) + Z), Z)
         x_ = 1 - x if w == 0 else x
         start = pl.multiple_of(x_ * (8 * Z) + z_ * 8, 8)
@@ -246,7 +268,7 @@
         lax.fori_loop(p * PIECE, (p + 1) * PIECE, body, 0)
 
     def r_x(j):
-        return remote(xsend.at[j], xrecv.at[j], rxs.at[j], rxr.at[j], over)
+        return remote(xsend.at[j], xrecv.at[j], rxs.at[j], rxr.at[j], askew if j % 2 else over)
 
     def r_over(p):
         r_c(0, p).wait_recv()
@@ -255,21 +277,12 @@
             send(r_x(j))
 
     def hop_of(k):
-        size = abs(k)
-        step = (size - 1) % reach + 1
-        return step if k > 0 else -step
+        return k - before(WAY_R, k)
 
     def r_z(k):
         return remote(zsend.at[k % Z], zrecv.at[k % Z], rzs.at[k % Z], rzr.at[k % Z], along(hop_of(k)))
 
     waited = set()
-
-    def feeds(k):
-        out = []
-        for k_ in plus + minus:
-            if k_ - hop_of(k_) == k:
-                out.append(k_)
-        return out
 
     def r_sum(k):
         j = place[k]
@@ -279,7 +292,7 @@
             r_c(1, p).wait_recv()
         r_x(j).wait_recv()
         total = own[1, j] + crecv[1, j].astype(F32) + xrecv[j].astype(F32)
-        for k_ in feeds(k):
+        for k_ in after(WAY_R, k):
             r_z(k_).wait_recv()
             total += zrecv[k_ % Z].astype(F32)
         return total
@@ -352,20 +365,18 @@
     def add(time, what, *args):
         events.append((time, len(events), what, args))
 
-    step_time = 3.6 if reach <= 2 else 5.0
-    x_time = 1.0
-    z_ready = {0: 2.0}
+    z_ready = {0: A_FIRST}
     for k in plus + minus:
-        ready = 2.0 + step_time * (-(-abs(k) // reach)) + 0.1 * abs(k)
-        z_ready[k] = ready
-        add(ready, a_got_z, k)
+        z_ready[k] = z_ready[before(WAY_A, k)] + A_STEP + A_HOP * abs(k - before(WAY_A, k))
+        add(z_ready[k], a_got_z, k)
     c_ready = {}
-    for k in [0] + plus + minus:
-        ready = z_ready[k] + 4.5
+    for i, k in enumerate([0] + [k for pair in zip(plus, minus + [None]) for k in pair if k is not None]):
+        cross = max(z_ready[k] + 0.01, A_CROSS + A_EACH * i)
+        add(cross, a_cross, k)
+        ready = max(cross + A_OVER, A_LATE + A_LATER * i)
         add(ready, a_got_x, k)
-        c_ready[k] = ready + 2.0
-        add(c_ready[k], a_got_c, k) if k else add(c_ready[k], arrived_c, 1, 0)
-    add(c_ready[0] - 0.5, arrived_c, 0, 0)
+        c_ready[k] = ready + A_BESIDE
+        add(c_ready[k], a_got_c, k)
     last = 0.0
     for j in range(half):
         rel = j if j <= half // 2 else j - half
@@ -375,11 +386,11 @@
         add(ready, unfold, rel)
     r_ready = {}
     for p in range(pieces):
-        add(5.0 + 0.3 * p, r_over, p)
+        add(R_OVER + R_PIECE * p, r_over, p)
     for k in order:
-        ready = 8.0 + x_time * place[k]
-        for k_ in feeds(k):
-            ready = max(ready, r_ready[k_] + step_time)
+        ready = R_FIRST + R_CHUNK * place[k]
+        for k_ in after(WAY_R, k):
+            ready = max(ready, r_ready[k_] + R_STEP + R_HOP * abs(hop_of(k_)))
         r_ready[k] = ready
         if k:
             add(ready, r_send, k)

time: 52.5 us -> 45.8 us (0.87)
  Pallas kernels: 50.3 us -> 44.1 us
    pallas_call x1, Pallas kernels: 49.6 us -> 43.4 us  [shards(): pl.pallas_call(functools.partial(kernel, NG, Z, tokens_all), out_shape=(V...]
where the time goes in v3:
time: 45.8 us; the launch traced here: 45.4 us
  Pallas kernels  44.1 us (96%)
  between operations  1.29 us (3%)
    pallas_call x1, Pallas kernels, shards(): pl.pallas_call(functools.partial(kernel, NG, Z, tokens_all), out_shape=(V...  43.4 us

profile of v3, /device:TPU:1, one launch (start us, length us, event | category | flops | bytes accessed | tf_op | source)
XLA Modules:
  0.0 45.4 jit_solution(17427232422561718731)
XLA Ops:
  1.3 43.4 %step.1 = (bf16[384,256]{1,0:T(8,128)(2,1)S(1)}, f32[128,128]{1,0:T(8,128)S(1)}, f32[128,128]{1,0:T(8,128)S(1)}, f32[128,128]{1,0:T(8,128)S(1)}) custom-call(s32[1]{0:T(128)S(6)} %copy.10.step_ref, bf16[384,256]{1,0:T(8,128)(2,1)} %bitcast.10, bf16[384,4096]{1,0:T(8,128)(2,1)} %bitcast.9, f32[128,128]{1,0:T(8,128)} %bitcast.11, f32[128,128]{1,0:T(8,128)} %bitcast.12, ...), custom_call_target="tpu_custom_call" | custom-call | tf_op jit(solution)/shard_map/step/pallas_call | solution.py:427
  44.6 0.8 %store.1 = (bf16[384,256]{1,0:T(8,128)(2,1)}, f32[128,128]{1,0:T(8,128)}, f32[128,128]{1,0:T(8,128)}, f32[128,128]{1,0:T(8,128)}) custom-call(bf16[384,256]{1,0:T(8,128)(2,1)S(1)} %get-tuple-element.12.refs_0_, f32[128,128]{1,0:T(8,128)S(1)} %get-tuple-element.13.refs_1_, f32[128,128]{1,0:T(8,128)S(1)} %get-tuple-element.14.refs_2_, ...), custom_call_target="tpu_custom_call" | custom-call | tf_op jit(solution)/shard_map/store/pallas_call | solution.py:448

commit v4 on v3

--- a/solution.py
+++ b/solution.py
@@ -33,7 +33,7 @@
 A_LATER = 0.4
 R_STEP = 2.4
 R_HOP = 0.7
-R_FIRST = 6.5
+R_FIRST = 7.5
 R_CHUNK = 0.6
 R_OVER = 3.3
 R_PIECE = 0.2
@@ -54,7 +54,7 @@
     grad_out, master_out, one_out, two_out,
     ctx, up, master, one, two,
     gsum, own, csend, crecv, xsend, xrecv, zsend, zrecv,
-    wbuf, wmat, cg, folded, stepped, sent, got,
+    wbuf, wmat, folded, stepped, sent, got,
     in_sem,
     azs, azr, axs, axr, acs, acr,
     rcs, rcr, rxs, rxr, rzs, rzr, gs, gr,
@@ -73,8 +73,8 @@
     def at(x_, z_, c_):
         return (group, x_ * (2 * Z) + z_ * 2 + c_)
 
-    def along(k):
-        return at(x, lax.rem(z + (k + 2 * Z), Z), c)
+    def along(k, core=None):
+        return at(x, lax.rem(z + (k + 2 * Z), Z), c if core is None else core)
 
     over = at(1 - x, z, c)
     askew = at(1 - x, z, 1 - c)
@@ -104,8 +104,13 @@
     def after(way, k):
         return sorted((n for n in plus + minus if before(way, n) == k), key=lambda n: -abs(n))
 
-    hops = sorted({(k - before(way, k)) % Z for way in (WAY_A, WAY_R) for k in plus + minus})
-    peers = [along(h) for h in hops] + [over, askew, beside] + partners
+    def hops(way):
+        return sorted({(k - before(way, k)) % Z for k in plus + minus})
+
+    def steps(k):
+        return 0 if k == 0 else 1 + steps(before(WAY_R, k))
+
+    peers = [along(h) for h in hops(WAY_A)] + [along(h, 1 - c) for h in hops(WAY_R)] + [over, askew, beside] + partners
     barrier = pltpu.get_barrier_semaphore()
     for peer in peers:
         pl.semaphore_signal(barrier, inc=1, device_id=peer, device_id_type=MESH)
@@ -211,20 +216,8 @@
                 wmat[pl.ds(start, 16), pl.ds(q * Q, Q)] = jnp.concatenate(outs[q], 0).astype(BF16)
 
     def multiply():
-        for q in range(PARTS):
-            part = lax.dot_general(
-                up[:, pl.ds(q * Q, Q)], wmat[:, pl.ds(q * Q, Q)],
-                (((1,), (1,)), ((), ())), preferred_element_type=F32,
-            )
-            if q == 0:
-                cg[...] = part
-            elif q < PARTS - 1:
-                cg[...] += part
-            else:
-                grad_out[...] = (cg[...] + part).astype(BF16)
-
-    def offset(j):
-        return jnp.where(lax.rem(j, 2) == 1, half - (j + 1) // 2, (j // 2) - half)
+        total = lax.dot_general(up[...], wmat[...], (((1,), (1,)), ((), ())), preferred_element_type=F32)
+        grad_out[...] = total.astype(BF16)
 
     order = [half]
     for k in range(half - 1, 0, -1):
@@ -240,8 +233,9 @@
             gsum[q] = jnp.dot(turned, up[:, pl.ds(q * Q, Q)], preferred_element_type=F32)
 
     def fold(w, j):
-        first_core = lax.rem(c + j, 2) == 0 if w == 0 else c == 0
-        z_ = lax.rem(z + (offset(j) + Z), Z)
+        turns = steps(order[j]) + (j if w == 0 else 0)
+        first_core = c == turns % 2
+        z_ = lax.rem(z + (order[j] + Z), Z)
         x_ = 1 - x if w == 0 else x
         start = pl.multiple_of(x_ * (8 * Z) + z_ * 8, 8)
         s = [gsum[q, pl.ds(start, 8), :] for q in range(PARTS)]
@@ -261,11 +255,8 @@
         return remote(csend.at[w, part], crecv.at[w, part], rcs.at[w, p], rcr.at[w, p], beside)
 
     def r_fold(w, p):
-        def body(j, carry):
+        for j in range(p * PIECE, (p + 1) * PIECE):
             fold(w, j)
-            return carry
-
-        lax.fori_loop(p * PIECE, (p + 1) * PIECE, body, 0)
 
     def r_x(j):
         return remote(xsend.at[j], xrecv.at[j], rxs.at[j], rxr.at[j], askew if j % 2 else over)
@@ -280,7 +271,7 @@
         return k - before(WAY_R, k)
 
     def r_z(k):
-        return remote(zsend.at[k % Z], zrecv.at[k % Z], rzs.at[k % Z], rzr.at[k % Z], along(hop_of(k)))
+        return remote(zsend.at[k % Z], zrecv.at[k % Z], rzs.at[k % Z], rzr.at[k % Z], along(hop_of(k), 1 - c))
 
     waited = set()
 
@@ -351,14 +342,12 @@
 
     make_chunk()
     product()
+    pl.semaphore_wait(barrier, len(peers))
+    a_start()
     for w in range(2):
         for p in range(pieces):
             r_fold(w, p)
-    pl.semaphore_wait(barrier, len(peers))
-    for w in range(2):
-        for p in range(pieces):
             send(r_c(w, p))
-    a_start()
 
     events = []
 
@@ -433,7 +422,7 @@
             V((T, rows), BF16), V((T, D), BF16), V((flat, 128), F32), V((flat, 128), F32), V((flat, 128), F32),
             V((PARTS, rows, Q), F32), V((2, Z) + chunk, F32), V((2, Z) + chunk, BF16), V((2, Z) + chunk, BF16),
             V((Z,) + chunk, BF16), V((Z,) + chunk, BF16), V((Z,) + chunk, BF16), V((Z,) + chunk, BF16),
-            V((2, 2, Z) + chunk, BF16), V((rows, D), BF16), V((T, rows), F32),
+            V((2, 2, Z) + chunk, BF16), V((rows, D), BF16),
             V((flat, 128), F32), V((flat, 128), F32), V((flat, 128), BF16), V((bits, flat, 128), BF16),
             DMA((4 + PARTS,)),
             DMA((Z,)), DMA((Z,)), DMA((Z,)), DMA((Z,)), DMA((2, Z)), DMA((2, Z)),

time: 45.8 us -> 45.2 us (0.987)
  no operation moved by 1% of the time
where the time goes in v4:
time: 45.2 us; the launch traced here: 45 us
  Pallas kernels  43.7 us (97%)
  between operations  1.29 us (3%)
    pallas_call x1, Pallas kernels, shards(): pl.pallas_call(functools.partial(kernel, NG, Z, tokens_all), out_shape=(V...  43 us

profile of v4, /device:TPU:1, one launch (start us, length us, event | category | flops | bytes accessed | tf_op | source)
XLA Modules:
  0.0 45.0 jit_solution(14473345431160109771)
XLA Ops:
  1.3 43.0 %step.1 = (bf16[384,256]{1,0:T(8,128)(2,1)S(1)}, f32[128,128]{1,0:T(8,128)S(1)}, f32[128,128]{1,0:T(8,128)S(1)}, f32[128,128]{1,0:T(8,128)S(1)}) custom-call(s32[1]{0:T(128)S(6)} %copy.10.step_ref, bf16[384,256]{1,0:T(8,128)(2,1)} %bitcast.10, bf16[384,4096]{1,0:T(8,128)(2,1)} %bitcast.9, f32[128,128]{1,0:T(8,128)} %bitcast.11, f32[128,128]{1,0:T(8,128)} %bitcast.12, ...), custom_call_target="tpu_custom_call" | custom-call | tf_op jit(solution)/shard_map/step/pallas_call | solution.py:416
  44.3 0.8 %store.1 = (bf16[384,256]{1,0:T(8,128)(2,1)}, f32[128,128]{1,0:T(8,128)}, f32[128,128]{1,0:T(8,128)}, f32[128,128]{1,0:T(8,128)}) custom-call(bf16[384,256]{1,0:T(8,128)(2,1)S(1)} %get-tuple-element.12.refs_0_, f32[128,128]{1,0:T(8,128)S(1)} %get-tuple-element.13.refs_1_, f32[128,128]{1,0:T(8,128)S(1)} %get-tuple-element.14.refs_2_, ...), custom_call_target="tpu_custom_call" | custom-call | tf_op jit(solution)/shard_map/store/pallas_call | solution.py:437
